TPU v7x, 32 devices: a whole 2x2x4 slice. The times are simulated.
32 devices in a mesh: pipe: 4 (over y, core), expert: 8 (over z, x).
Axes of the slice: x: 2, y: 2, z: 4, core: 2. Of those that a mesh axis runs over, the one named last changes fastest.
Arguments:
- saved_inputs: bfloat16 [4, 1024, 2048], P('pipe', 'expert'), may hold values from -6 to 6
- grad_out: bfloat16 [4, 1024, 2048], P('pipe', 'expert'), may hold values from -6 to 6
- routes: int32 [4, 1024, 8], P('pipe', 'expert'), may hold values from 0 to 31, all different within a row; in each aligned block of 128 rows (0 to 127, 128 to 255, ..., all dimensions but the last counted through in order) at most 36 rows name the same one
- route_probs: float32 [4, 1024, 8], P('pipe', 'expert'), may hold values from 0.1 to 0.6
- w_in: bfloat16 [4, 32, 2048, 768], P('pipe', 'expert'), may hold values from -0.125 to 0.125
- w_out: bfloat16 [4, 32, 384, 2048], P('pipe', 'expert'), may hold values from -0.3125 to 0.3125
Outputs:
- grad_tokens: float32 [4, 1024, 2048], P('pipe', 'expert')
- grad_w_in: bfloat16 [4, 32, 2048, 768], P('pipe', 'expert')
- grad_w_out: bfloat16 [4, 32, 384, 2048], P('pipe', 'expert')
Inputs may be any that keep to these rules, and one draw needn't show every extreme that they name: `routes`: each row names 8 different experts. Among the rows of one device (aligned blocks of 128 rows) no expert is named more than 36 times, a bound that some block reaches.
All inputs are finite; a program needn't handle non-finite values.
Results may differ from a plain program's by a relative error of at most 0.0057.
Values may be sent and summed in bfloat16 or wider, within the bound.
A program may use at most 128 MiB of HBM per device.

v0:
```python
import jax
import jax.numpy as jnp
from jax import lax
from jax.sharding import PartitionSpec as P

CAP = 36


def swapped(block, axis, stride):
    count = lax.axis_size(axis)
    route = []
    for low in range(count):
        high = low | 1 << stride
        if high != low and high < count:
            route += [(low, high), (high, low)]
    return lax.ppermute(block, axis, route)


def silu_parts(gates):
    sigma = jax.nn.sigmoid(gates)
    return (gates * sigma, sigma * (1.0 + gates * (1.0 - sigma)))


def slot_table(route_ids, route_weights, first, count, capacity):
    tok_count, top_count = route_ids.shape
    flat_ids = route_ids.reshape(-1)
    expert_ids = first + jnp.arange(count, dtype=jnp.int32)
    onehot = (flat_ids[:, None] == expert_ids[None, :]).astype(jnp.int32)
    ranks = jnp.cumsum(onehot, axis=0) - 1
    slots = jnp.sum(onehot * ranks, axis=1)
    local_ids = jnp.sum(onehot * jnp.arange(count, dtype=jnp.int32)[None, :], axis=1)
    hits = jnp.sum(onehot, axis=1)
    dest = jnp.where(hits > 0, local_ids * capacity + slots, count * capacity)
    token_ids = jnp.arange(tok_count * top_count, dtype=jnp.int32) // top_count
    table = (
        jnp.full((count * capacity + 1,), -1, jnp.int32).at[dest].set(token_ids)[: count * capacity]
    )
    weight = (
        jnp.zeros((count * capacity + 1,), jnp.float32)
        .at[dest]
        .set(route_weights.reshape(-1))[: count * capacity]
    )
    return (table, weight, dest)


def pick_rows(input_rows, grad_rows, table, weight):
    valid = table >= 0
    safe_index = jnp.maximum(table, 0)
    picked = jnp.where(valid[:, None], input_rows[safe_index], jnp.zeros((), input_rows.dtype))
    scaled = (weight[:, None] * grad_rows[safe_index].astype(jnp.float32)).astype(jnp.bfloat16)
    return (picked, scaled)


def per_device(saved_inputs, grad_out, routes, route_probs, w_in, w_out):
    pipe_count = lax.axis_size("pipe")
    owner_count = lax.axis_size("expert")
    own_saved = saved_inputs[0]
    tok_count, width = own_saved.shape
    section_in = own_saved
    for bit_index in range(pipe_count.bit_length() - 1):
        section_in = swapped(section_in, "pipe", bit_index)
    section_grad = grad_out[0]
    own_routes = routes[0]
    own_probs = route_probs[0]
    top_count = own_routes.shape[1]
    weight_in = w_in[0]
    weight_out = w_out[0]
    local_experts = weight_in.shape[0]
    hidden_units = weight_out.shape[1]
    all_experts = local_experts * owner_count
    table, weight, dest = slot_table(own_routes, own_probs, 0, all_experts, CAP)
    every_in, every_grad = (
        lax.all_gather(section_in, "expert", axis=0, tiled=True),
        lax.all_gather(section_grad, "expert", axis=0, tiled=True),
    )
    every_routes = lax.all_gather(own_routes, "expert", axis=0, tiled=True)
    every_probs = lax.all_gather(own_probs, "expert", axis=0, tiled=True)
    first_expert = lax.axis_index("expert") * local_experts
    tables, weights, unused = jax.vmap(
        lambda ids, probs: slot_table(ids, probs, first_expert, local_experts, CAP)
    )(
        every_routes.reshape(owner_count, tok_count, top_count),
        every_probs.reshape(owner_count, tok_count, top_count),
    )
    offsets = (jnp.arange(owner_count, dtype=jnp.int32) * tok_count)[:, None]
    global_table = jnp.where(tables >= 0, tables + offsets, -1).reshape(-1)
    got_in, got_grad = pick_rows(every_in, every_grad, global_table, weights.reshape(-1))
    rows_in = got_in.reshape(owner_count, local_experts, CAP, width)
    rows_grad = got_grad.reshape(owner_count, local_experts, CAP, width)
    gate_up = jnp.einsum("secd,edf->secf", rows_in, weight_in, preferred_element_type=jnp.float32)
    gates = gate_up[..., :hidden_units]
    upper = gate_up[..., hidden_units:]
    active, slope = silu_parts(gates)
    hidden = (active * upper).astype(jnp.bfloat16)
    hidden_grad = jnp.einsum(
        "secd,efd->secf", rows_grad, weight_out, preferred_element_type=jnp.float32
    )
    pre_grad = jnp.concatenate([hidden_grad * upper * slope, hidden_grad * active], axis=3).astype(
        jnp.bfloat16
    )
    grad_out_w = jnp.einsum(
        "secf,secd->efd", hidden, rows_grad, preferred_element_type=jnp.float32
    ).astype(jnp.bfloat16)
    grad_in_w = jnp.einsum(
        "secd,secf->edf", rows_in, pre_grad, preferred_element_type=jnp.float32
    ).astype(jnp.bfloat16)
    row_grads = jnp.einsum(
        "secf,edf->secd", pre_grad, weight_in, preferred_element_type=jnp.float32
    ).astype(jnp.bfloat16)
    back_rows = lax.all_to_all(
        row_grads.reshape(owner_count * local_experts * CAP, width),
        "expert",
        split_axis=0,
        concat_axis=0,
        tiled=True,
    )
    gathered = back_rows[dest].astype(jnp.float32).reshape(tok_count, top_count, width)
    token_grads = jnp.sum(gathered, axis=1)
    return (token_grads[None], grad_in_w[None], grad_out_w[None])


def solution(mesh):
    in_specs = (
        P("pipe", "expert", None),
        P("pipe", "expert", None),
        P("pipe", "expert", None),
        P("pipe", "expert", None),
        P("pipe", "expert", None, None),
        P("pipe", "expert", None, None),
    )
    out_specs = (
        P("pipe", "expert", None),
        P("pipe", "expert", None, None),
        P("pipe", "expert", None, None),
    )
    return jax.shard_map(
        per_device, mesh=mesh, in_specs=in_specs, out_specs=out_specs, check_vma=False
    )
```

profile of v0, /device:TPU:0, one launch (start us, length us, event | category | flops | bytes accessed | tf_op | source)
XLA Modules:
  0.0 374.6 jit_solution(51678568004038895)
XLA Ops:
  7.2 0.7 all-gather.8.cloned.1.call-update
  8.0 0.5 collective-permute-start
  8.5 1.7 collective-permute-done
  10.2 2.9 collective-permute-start.1
  13.1 12.2 %collective-permute-done.1 = bf16[128,2048]{1,0:T(8,128)(2,1)S(1)} collective-permute-done((bf16[128,2048]{1,0:T(8,128)(2,1)S(1)}, bf16[128,2048]{1,0:T(8,128)(2,1)S(1)}, u32[]{:S(2)}, u32[]{:S(2)}) %collective-permute-start.1) | collective-permute-done | bytes 524320 | tf_op jit(solution)/shard_map/ppermute | solution.py:16
  25.4 0.8 copy-done
  26.2 31.4 %all-gather = s32[1,1024,8]{1,2,0:T(8,128)S(1)} all-gather(s32[1,128,8]{1,2,0:T(8,128)} %param.8), channel_id=2, replica_groups=mesh['pipe'=4,'expert'=8] {'expert'}, dimensions={1}, use_global_device_ids=true | all-gather | bytes 36864 | tf_op jit(solution)/shard_map/all_gather | solution.py:76
  57.8 0.3 eq.56
  58.0 0.3 eq.52
  58.4 9.0 %reduce-window.14 = s32[8,4,8,128]{3,2,1,0:T(8,128)S(1)} reduce-window(s32[8,4,8,128]{3,2,1,0:T(8,128)S(1)} %compare_convert_fusion.1, s32[]{:T(128)} %constant.25.clone.1), window={size=1x1x1x128 pad=0_0x0_0x0_0x127_0}, to_apply=%region_2.3 | reduce-window | flops 4161536 | bytes 262148 | tf_op jit(solution)/shard_map/reduce-window
  67.6 0.3 copy.28
  67.8 0.6 reduce-window.15
  68.6 0.3 fusion.24
  69.2 30.4 %scatter_custom_fusion.1 = s32[1160]{0:T(1024)S(1)} fusion(s32[8192]{0:T(1024)S(1)} %bitcast.102, s32[8192]{0:T(1024)S(1)} %bitcast.101, s32[]{:T(128)} %constant.29.clone.1), kind=kCustom, calls=%fused_computation.69 | custom fusion | bytes 4644
  100.1 30.7 %all-gather.1 = f32[1,1024,8]{1,2,0:T(8,128)S(1)} all-gather(f32[1,128,8]{1,2,0:T(8,128)S(1)} %copy-done.2), channel_id=3, replica_groups=mesh['pipe'=4,'expert'=8] {'expert'}, dimensions={1}, use_global_device_ids=true | all-gather | bytes 36864 | tf_op jit(solution)/shard_map/all_gather | solution.py:77
  131.3 30.4 %scatter_custom_fusion = f32[1160]{0:T(1024)S(1)} fusion(s32[8192]{0:T(1024)S(1)} %bitcast.103, f32[8192]{0:T(1024)S(1)} %reshape.210, f32[]{:T(128)} %constant.22.clone.1), kind=kCustom, calls=%fused_computation.71 | custom fusion | bytes 4644
  161.9 13.9 %gather_fusion = bf16[1152,2048]{1,0:T(8,128)(2,1)} fusion(bf16[1024,2048]{1,0:T(8,128)(2,1)} %bitcast.92, s32[2048]{0:T(1024)S(1)} %pad_clamp_fusion), kind=kCustom, calls=%fused_computation | custom fusion | bytes 9441792 | tf_op jit(solution)/shard_map/gather | solution.py:50
  175.8 7.9 %reshape.182 = f32[8,4,36,2048]{3,2,1,0:T(8,128)} reshape(bf16[1152,2048]{1,0:T(8,128)(2,1)} %gather_fusion) | data formatting | bytes 14155776 | tf_op jit(solution)/shard_map/convert_element_type | solution.py:50
  183.7 13.4 %gather_fusion.1 = bf16[1152,2048]{1,0:T(8,128)(2,1)} fusion(bf16[1024,2048]{1,0:T(8,128)(2,1)} %all-gather.6.cloned.1.call-done, s32[2048]{0:T(1024)S(1)} %pad_clamp_fusion), kind=kCustom, calls=%fused_computation.1 | custom fusion | bytes 9441792 | tf_op jit(solution)/shard_map/gather | solution.py:49
  197.1 7.2 %gather.13 = bf16[8,4,36,2048]{3,2,1,0:T(8,128)(2,1)} reshape(bf16[1152,2048]{1,0:T(8,128)(2,1)} %gather_fusion.1) | data formatting | bytes 9437184 | tf_op jit(solution)/shard_map/gather | solution.py:49
  204.3 12.4 %fusion.13 = f32[8,4,36,768]{3,2,0,1:T(8,128)} fusion(bf16[1,4,2048,768]{3,2,1,0:T(8,128)(2,1)} %param.10, bf16[8,4,36,2048]{3,2,1,0:T(8,128)(2,1)} %gather.13, pred[8,4,36]{2,1,0:T(4,128)(4,1)S(1)} %ge.19), kind=kOutput, calls=%fused_computation.22 | convolution fusion | flops 3626237952 | bytes 20841600 | tf_op jit(solution)/shard_map/secd,edf->secf/dot_general | solution.py:90
  216.7 10.6 %fusion.19 = (bf16[8,4,36,384]{3,2,0,1:T(8,128)(2,1)S(1)}, bf16[8,4,36,384]{3,2,0,1:T(8,128)(2,1)S(1)}) fusion(f32[8,4,36,768]{3,2,0,1:T(8,128)} %fusion.13, bf16[1,4,384,2048]{3,2,1,0:T(8,128)(2,1)} %param.11, f32[8,4,36,2048]{3,2,1,0:T(8,128)} %reshape.182, f32[8,4,36]{2,1,0:T(4,128)S(1)} %mul.96), kind=kOutput, calls=%fused_computation.27 | convolution fusion | flops 1822408704 | bytes 21041664 | tf_op jit(solution)/shard_map/secd,efd->secf/dot_general | solution.py:95
  227.2 14.7 %convert_bitcast_fusion = bf16[8,4,36,2048]{3,2,0,1:T(8,128)(2,1)} fusion(bf16[1,4,2048,768]{3,2,1,0:T(8,128)(2,1)} %param.10, bf16[8,4,36,384]{3,2,0,1:T(8,128)(2,1)S(1)} %get-tuple-element.10, bf16[8,4,36,384]{3,2,0,1:T(8,128)(2,1)S(1)} %get-tuple-element.9), kind=kOutput, calls=%fused_computation.18 | convolution fusion | flops 3629776896 | bytes 19070976 | tf_op jit(solution)/shard_map/secf,edf->secd/dot_general | solution.py:107
  241.9 5.2 %copy.33 = bf16[8,4,36,2048]{3,0,2,1:T(8,128)(2,1)S(1)} copy(bf16[8,4,36,2048]{3,2,0,1:T(8,128)(2,1)} %convert_bitcast_fusion) | data formatting | bytes 9437184 | tf_op jit(solution)/shard_map/convert_element_type | solution.py:109
  247.1 4.8 %copy.34 = bf16[8,144,2048]{2,1,0:T(8,128)(2,1)} copy(bf16[8,144,2048]{2,0,1:T(8,128)(2,1)S(1)} %bitcast.93) | data formatting | bytes 9437184 | tf_op jit(solution)/shard_map/all_to_all | solution.py:110
  251.9 5.9 %all-to-all-start = ((bf16[8,144,2048]{2,1,0:T(8,128)(2,1)}), bf16[8,144,2048]{2,1,0:T(8,128)(2,1)}, u32[]{:S(2)}, u32[]{:S(2)}) async-start(bf16[8,144,2048]{2,1,0:T(8,128)(2,1)} %copy.34), calls=%async_computation | async-start | bytes 9437184 | tf_op jit(solution)/shard_map/all_to_all | solution.py:110
  258.1 9.0 %reduce-window.16 = s32[32,8,128]{2,1,0:T(8,128)S(1)} reduce-window(s32[32,8,128]{2,1,0:T(8,128)S(1)} %fusion.29, s32[]{:T(128)} %constant.25.clone.1), window={size=1x1x128 pad=0_0x0_0x127_0}, to_apply=%region_9.10 | reduce-window | flops 4161536 | bytes 262148 | tf_op jit(solution)/shard_map/reduce-window.2
  267.7 11.9 %fusion.5 = bf16[1,4,384,2048]{3,2,1,0:T(8,128)(2,1)} fusion(f32[8,4,36,768]{3,2,0,1:T(8,128)} %fusion.13, f32[8,4,36,2048]{3,2,1,0:T(8,128)} %reshape.182, f32[8,4,36]{2,1,0:T(4,128)S(1)} %mul.96), kind=kOutput, calls=%fused_computation.14 | convolution fusion | flops 1822457856 | bytes 19272192 | tf_op jit(solution)/shard_map/secf,secd->efd/dot_general | solution.py:101
  279.6 10.2 %fusion = bf16[1,4,2048,768]{3,2,1,0:T(8,128)(2,1)} fusion(bf16[8,4,36,2048]{3,2,1,0:T(8,128)(2,1)S(1)} %bitcast.95, pred[8,4,36]{2,1,0:T(4,128)(4,1)S(1)} %ge.19, bf16[8,4,36,384]{3,2,0,1:T(8,128)(2,1)S(1)} %get-tuple-element.10, bf16[8,4,36,384]{3,2,0,1:T(8,128)(2,1)S(1)} %get-tuple-element.9), kind=kOutput, calls=%fused_computation.6 | convolution fusion | flops 3636068352 | bytes 19072128 | tf_op jit(solution)/shard_map/secd,secf->edf/dot_general | solution.py:104
  289.8 59.6 %all-to-all-done = bf16[8,144,2048]{2,1,0:T(8,128)(2,1)} async-done(((bf16[8,144,2048]{2,1,0:T(8,128)(2,1)}), bf16[8,144,2048]{2,1,0:T(8,128)(2,1)}, u32[]{:S(2)}, u32[]{:S(2)}) %all-to-all-start) | async-done | bytes 4718624 | tf_op jit(solution)/shard_map/all_to_all | solution.py:110
  349.4 12.0 %gather_fusion.2 = bf16[1024,2048]{1,0:T(8,128)(2,1)} fusion(bf16[1152,2048]{1,0:T(8,128)(2,1)} %bitcast.15, s32[1024]{0:T(1024)S(1)} %broadcast_clamp_fusion), kind=kCustom, calls=%fused_computation.2 | custom fusion | bytes 8392704 | tf_op jit(solution)/shard_map/gather | solution.py:117
  361.5 6.0 %convert_reduce_fusion = f32[128,2048]{1,0:T(8,128)} fusion(bf16[1024,2048]{1,0:T(8,128)(2,1)} %gather_fusion.2), kind=kLoop, calls=%fused_computation.13 | loop fusion | flops 3932160 | bytes 5242880 | tf_op jit(solution)/shard_map/reduce_sum | solution.py:118
  (60 shorter events, 2.7 us)
Async XLA Ops:
  7.2 61.8 %copy-start.4 = (s32[2]{0:T(128)S(1)}, s32[2]{0:T(128)}, u32[]{:S(2)}) copy-start(s32[2]{0:T(128)} %constant.72) | copy-start | bytes 28
  7.2 61.9 %copy-start.3 = (s32[2]{0:T(128)S(1)}, s32[2]{0:T(128)}, u32[]{:S(2)}) copy-start(s32[2]{0:T(128)} %constant.75) | copy-start | bytes 28
  7.2 92.9 %copy-start.2 = (f32[1,128,8]{1,2,0:T(8,128)S(1)}, f32[1,128,8]{1,2,0:T(8,128)}, u32[]{:S(2)}) copy-start(f32[1,128,8]{1,2,0:T(8,128)} %param.9) | copy-start | bytes 12292
  7.2 154.7 %all-gather.8.cloned.1.call-start = ((), (), s32[]{:S(2)}) async-start(), calls=%async_computation.2 | async-start | bytes 4718592 | tf_op jit(solution)/shard_map/all_gather | solution.py:74
  7.9 175.8 %all-gather.6.cloned.1.call-start = ((), (), s32[]{:S(2)}) async-start(), calls=%async_computation.1 | async-start | bytes 4718592 | tf_op jit(solution)/shard_map/all_gather | solution.py:73
  8.0 2.3 collective-permute-start
  10.2 15.1 %collective-permute-start.1 = (bf16[128,2048]{1,0:T(8,128)(2,1)S(1)}, bf16[128,2048]{1,0:T(8,128)(2,1)S(1)}, u32[]{:S(2)}, u32[]{:S(2)}) collective-permute-start(bf16[128,2048]{1,0:T(8,128)(2,1)S(1)} %collective-permute-done), channel_id=1, source_target_pairs={{0,16},{16,0},{8,24},{24,8},{1,17},{17,1},{9,25},{25,9},{2,18},{18... | collective-permute-start | bytes 1572872 | tf_op jit(solution)/shard_map/ppermute | solution.py:16
  25.4 0.8 copy-start
  251.9 5.9 %copy-start.1 = (s32[1,128,8]{1,2,0:T(8,128)S(1)}, s32[1,128,8]{1,2,0:T(8,128)}, u32[]{:S(2)}) copy-start(s32[1,128,8]{1,2,0:T(8,128)} %param.8) | copy-start | bytes 12292
  251.9 27.7 %slice-start = ((s8[5242880]{0:T(1024)(128)(4,1)}), s8[1048576]{0:T(1024)(128)(4,1)S(1)}, s32[]{:S(2)}) async-start(s8[5242880]{0:T(1024)(128)(4,1)} %bitcast.94), calls=%async_computation.3 | async-start | bytes 2097152
  251.9 97.5 %all-to-all-start = ((bf16[8,144,2048]{2,1,0:T(8,128)(2,1)}), bf16[8,144,2048]{2,1,0:T(8,128)(2,1)}, u32[]{:S(2)}, u32[]{:S(2)}) async-start(bf16[8,144,2048]{2,1,0:T(8,128)(2,1)} %copy.34), calls=%async_computation | async-start | bytes 9437184 | tf_op jit(solution)/shard_map/all_to_all | solution.py:110
  267.7 11.9 %slice-start.1 = ((s8[5242880]{0:T(1024)(128)(4,1)}), s8[4194304]{0:T(1024)(128)(4,1)S(1)}, s32[]{:S(2)}) async-start(s8[5242880]{0:T(1024)(128)(4,1)} %bitcast.94), calls=%async_computation.4 | async-start | bytes 8388608
Sparse Core Ops, SparseCore 0:
  10.2 76.3 all-gather.7
  89.2 71.9 all-gather.5
where the time goes:
time: 379 us; the launch traced here: 375 us
  local copies, waits for them, and re-layouts  129 us (34%)
  waiting for transfers between devices  74.3 us (20%)
  blocking collectives  62.1 us (16%)
  matrix products  59.7 us (16%)
  other arithmetic  25.7 us (7%)
  between operations  14.6 us (4%)
  starting transfers between devices  9.37 us (2%)
    unnamed x21, local copies, waits for them, and re-layouts  61.8 us
    all_to_all x1, waiting for transfers between devices, per_device(): lax.all_to_all(row_grads.reshape(owner_count * local_experts * CAP, width...  59.6 us
    all_gather x1, blocking collectives, per_device(): every_routes = lax.all_gather(own_routes, 'expert', axis=0, tiled=True)  31.4 us
    all_gather x1, blocking collectives, per_device(): every_probs = lax.all_gather(own_probs, 'expert', axis=0, tiled=True)  30.7 us
    gather x2, local copies, waits for them, and re-layouts, pick_rows(): input_rows[safe_index]  20.6 us
    another operation x4, other arithmetic  18.7 us
    dot_general x1, matrix products, per_device(): jnp.einsum('secf,edf->secd', pre_grad, weight_in, preferred_element_type=...  14.7 us
    ppermute x2, waiting for transfers between devices, swapped(): return lax.ppermute(block, axis, route)  14 us
  transfers between devices with their start and end apart: 5, of which 3 were waited for; matrix products, arithmetic and copies ran while one was open for 34% of the time, Pallas kernels for 0%

commit v1 on v0

v1 whole, which is shorter than its diff:
```python
import jax
import jax.numpy as jnp
from jax import lax
from jax.sharding import PartitionSpec as P

CAP = 36


def swapped(block, axis):
    count = lax.axis_size(axis)
    return lax.ppermute(block, axis, [(i, count - 1 - i) for i in range(count)])


def silu_parts(gates):
    sigma = jax.nn.sigmoid(gates)
    return (gates * sigma, sigma * (1.0 + gates * (1.0 - sigma)))


def picks(meta, first, count, capacity, top):
    ids, probs = meta[..., :top], meta[..., top:]
    experts = (first + jnp.arange(count)).astype(jnp.float32)
    named = ids[:, None] == experts[None, :, None, None]
    hit = jnp.any(named, axis=-1)
    weight = jnp.sum(jnp.where(named, probs[:, None], 0.0), axis=-1)
    tokens = jnp.arange(ids.shape[1])
    earlier = (tokens[:, None] < tokens[None, :]).astype(jnp.bfloat16)
    rank = jnp.einsum("set,tu->seu", hit.astype(jnp.bfloat16), earlier, preferred_element_type=jnp.float32)
    slot = jnp.arange(capacity).astype(jnp.float32)
    pick = hit[:, :, None, :] & (rank[:, :, None, :] == slot[None, None, :, None])
    row_weight = jnp.sum(jnp.where(pick, weight[:, :, None, :], 0.0), axis=-1)
    return pick.astype(jnp.bfloat16), row_weight


def plain(saved_inputs, grad_out, routes, route_probs, w_in, w_out):
    owner_count = lax.axis_size("expert")
    weight_in, weight_out = w_in[0], w_out[0]
    local_experts, width, hidden2 = weight_in.shape
    hidden_units = hidden2 // 2
    tok_count, top = routes.shape[1:]
    meta = jnp.concatenate([routes[0].astype(jnp.float32), route_probs[0]], axis=1)
    every_meta = lax.all_gather(meta, "expert", axis=0)
    section_in = swapped(saved_inputs[0], "pipe")
    every_grad = lax.all_gather(grad_out[0], "expert", axis=0)
    every_in = lax.all_gather(section_in, "expert", axis=0)
    first = lax.axis_index("expert") * local_experts
    pick, row_weight = picks(every_meta, first, local_experts, CAP, top)
    f32 = jnp.float32
    rows_in = jnp.einsum("sect,std->secd", pick, every_in, preferred_element_type=f32).astype(jnp.bfloat16)
    rows_grad = jnp.einsum("sect,std->secd", pick, every_grad, preferred_element_type=f32)
    rows_grad = (rows_grad * row_weight[..., None]).astype(jnp.bfloat16)
    gate_up = jnp.einsum("secd,edf->secf", rows_in, weight_in, preferred_element_type=f32)
    gates, upper = gate_up[..., :hidden_units], gate_up[..., hidden_units:]
    active, slope = silu_parts(gates)
    hidden = (active * upper).astype(jnp.bfloat16)
    hidden_grad = jnp.einsum("secd,efd->secf", rows_grad, weight_out, preferred_element_type=f32)
    pre_grad = jnp.concatenate([hidden_grad * upper * slope, hidden_grad * active], axis=3).astype(jnp.bfloat16)
    row_grads = jnp.einsum("secf,edf->secd", pre_grad, weight_in, preferred_element_type=f32).astype(jnp.bfloat16)
    partial = jnp.einsum("sect,secd->std", pick, row_grads, preferred_element_type=f32).astype(jnp.bfloat16)
    back = lax.all_to_all(partial, "expert", split_axis=0, concat_axis=0, tiled=True)
    grad_out_w = jnp.einsum("secf,secd->efd", hidden, rows_grad, preferred_element_type=f32).astype(jnp.bfloat16)
    grad_in_w = jnp.einsum("secd,secf->edf", rows_in, pre_grad, preferred_element_type=f32).astype(jnp.bfloat16)
    token_grads = jnp.sum(back.astype(f32), axis=0)
    return (token_grads[None], grad_in_w[None], grad_out_w[None])


def solution(mesh):
    rows = P("pipe", "expert", None)
    weights = P("pipe", "expert", None, None)
    return jax.shard_map(
        plain, mesh=mesh, in_specs=(rows, rows, rows, rows, weights, weights),
        out_specs=(rows, weights, weights), check_vma=False,
    )
```

time: 379 us -> 311 us (0.82); the launches traced: 375 us -> 311 us
  local copies, waits for them, and re-layouts: 129 us -> 3.14 us
  waiting for transfers between devices: 74.3 us -> 182 us
  blocking collectives: 62.1 us -> 32 us
  other arithmetic: 25.7 us -> 5.96 us
  matrix products: 59.7 us -> 65.7 us
    all_gather x2, waiting for transfers between devices: 0.02 us -> 97.1 us  [the longest x1 68.5 us: plain(): every_in = lax.all_gather(section_in, 'expert', axis=0)]
    unnamed x21 -> x17, local copies, waits for them, and re-layouts: 61.8 us -> 3.13 us
    gather x4 -> x0, local copies, waits for them, and re-layouts: 46.5 us -> none  [the longest x2 20.6 us: pick_rows(): input_rows[safe_index]]
    all_gather x2 -> x1, blocking collectives: 62.1 us -> 32 us  [plain(): every_meta = lax.all_gather(meta, 'expert', axis=0)]
    another operation x4 -> x0, other arithmetic: 18.7 us -> none
    convert_element_type x2 -> x0, local copies, waits for them, and re-layouts: 13 us -> none  [the longest x1 7.88 us: pick_rows(): grad_rows[safe_index].astype(jnp.float32)]
    all_to_all x1, waiting for transfers between devices: 59.6 us -> 71.7 us  [plain(): lax.all_to_all(partial, 'expert', split_axis=0, concat_axis=0, tiled=True)]
    dot_general x5 -> x9, matrix products: 59.7 us -> 65.7 us  [the longest x1 14.5 us: plain(): jnp.einsum('secf,edf->secd', pre_grad, weight_in, preferred_element_type=...]
  transfers between devices with their start and end apart: 5 -> 4, of which waited for: 3 -> 4; matrix products, arithmetic and copies ran while one was open for 34% -> 9% of each run, Pallas kernels for 0% -> 0%
where the time goes in v1:
time: 311 us
  waiting for transfers between devices  182 us (59%)
  matrix products  65.7 us (21%)
  blocking collectives  32 us (10%)
  between operations  14.2 us (5%)
  starting transfers between devices  7.49 us (2%)
  other arithmetic  5.96 us (2%)
  local copies, waits for them, and re-layouts  3.14 us (1%)
    all_to_all x1, waiting for transfers between devices, plain(): lax.all_to_all(partial, 'expert', split_axis=0, concat_axis=0, tiled=True)  71.7 us
    all_gather x1, waiting for transfers between devices, plain(): every_in = lax.all_gather(section_in, 'expert', axis=0)  68.5 us
    all_gather x1, blocking collectives, plain(): every_meta = lax.all_gather(meta, 'expert', axis=0)  32 us
    all_gather x1, waiting for transfers between devices, plain(): every_grad = lax.all_gather(grad_out[0], 'expert', axis=0)  28.7 us
    dot_general x1, matrix products, plain(): jnp.einsum('secf,edf->secd', pre_grad, weight_in, preferred_element_type=...  14.5 us
    ppermute x1, waiting for transfers between devices, swapped(): return lax.ppermute(block, axis, [(i, count - 1 - i) for i in range(count)])  12.6 us
    dot_general x1, matrix products, plain(): jnp.einsum('secd,secf->edf', rows_in, pre_grad, preferred_element_type=f32)  10.2 us
    dot_general x1, matrix products, plain(): jnp.einsum('secf,secd->efd', hidden, rows_grad, preferred_element_type=f32)  10.2 us
  transfers between devices with their start and end apart: 4, of which 4 were waited for; matrix products, arithmetic and copies ran while one was open for 9% of the time, Pallas kernels for 0%

profile of v1, /device:TPU:0, one launch (start us, length us, event | category | flops | bytes accessed | tf_op | source)
XLA Modules:
  0.0 310.7 jit_solution(14930986401864606370)
XLA Ops:
  7.2 0.0 all-gather.5.cloned.1.call-start
  7.2 0.7 all-gather.5.cloned.1.call-update
  7.9 0.0 all-gather.7.cloned.1.call-start
  7.9 2.5 collective-permute-start
  10.4 12.6 %collective-permute-done = bf16[128,2048]{1,0:T(8,128)(2,1)S(1)} collective-permute-done((bf16[128,2048]{1,0:T(8,128)(2,1)}, bf16[128,2048]{1,0:T(8,128)(2,1)S(1)}, u32[]{:S(2)}, u32[]{:S(2)}) %collective-permute-start) | collective-permute-done | bytes 524320 | tf_op jit(solution)/shard_map/ppermute | solution.py:11
  23.0 0.8 copy-done.1
  23.8 0.0 all-gather.7.cloned.1.call-update
  23.9 0.7 convert_bitcast_fusion
  24.5 0.7 pad_maximum_fusion.1
  25.2 32.0 %all-gather = f32[1024,16]{0,1:T(8,128)S(1)} all-gather(f32[128,16]{0,1:T(8,128)S(1)} %pad_maximum_fusion.1), channel_id=2, replica_groups=mesh['pipe'=4,'expert'=8] {'expert'}, dimensions={0}, use_global_device_ids=true | all-gather | bytes 73728 | tf_op jit(solution)/shard_map/all_gather | solution.py:41
  57.3 0.1 compare_reduce_fusion
  57.5 0.1 fusion.38
  57.6 0.1 fusion.40
  57.7 0.4 select_reduce_fusion
  58.1 28.7 %all-gather.5.cloned.1.call-done = bf16[8,128,2048]{2,1,0:T(8,128)(2,1)} async-done(((bf16[1,128,2048]{2,1,0:T(8,128)(2,1)}), bf16[8,128,2048]{2,1,0:T(8,128)(2,1)}) %all-gather.5.cloned.1.call-update) | async-done | bytes 4194320 | tf_op jit(solution)/shard_map/all_gather | solution.py:43
  86.8 6.1 %multiply_convert_fusion = bf16[8,4,36,2048]{3,2,1,0:T(8,128)(2,1)} fusion(f32[8,4,36]{2,1,0:T(4,128)S(1)} %select_reduce_fusion, bf16[8,128,2048]{2,1,0:T(8,128)(2,1)} %all-gather.5.cloned.1.call-done, f32[8,4,128]{2,1,0:T(4,128)S(1)} %fusion.40, f32[36]{0:T(128)S(1)} %iota_convert_fusion, pred[8,4,128]{2,1,0:T(4,128)(4,1)S(1)} %compare_reduce_fusion), kind=kOutput, calls=%fused_computation.7 | convolution fusion | flops 608993280 | bytes 8938128 | tf_op jit(solution)/shard_map/sect,std->secd/dot_general | solution.py:49
  92.9 68.5 %all-gather.7.cloned.1.call-done = bf16[1024,2048]{1,0:T(8,128)(2,1)} async-done(((bf16[128,2048]{1,0:T(8,128)(2,1)}), bf16[1024,2048]{1,0:T(8,128)(2,1)}) %all-gather.7.cloned.1.call-update) | async-done | bytes 4194320 | tf_op jit(solution)/shard_map/all_gather | solution.py:44
  161.3 3.9 %convolution_convert_fusion = bf16[8,4,36,2048]{3,2,1,0:T(8,128)(2,1)S(1)} fusion(bf16[8,128,2048,1]{2,1,3,0:T(8,128)(2,1)} %bitcast.79, f32[8,4,128]{2,1,0:T(4,128)S(1)} %fusion.40, f32[36]{0:T(128)S(1)} %iota_convert_fusion, pred[8,4,128]{2,1,0:T(4,128)(4,1)S(1)} %compare_reduce_fusion), kind=kOutput, calls=%fused_computation.20 | convolution fusion | flops 606633984 | bytes 8933520 | tf_op jit(solution)/shard_map/sect,std->secd/dot_general | solution.py:48
  165.2 0.0 copy-start
  165.2 2.3 copy-done
  167.5 7.4 %fusion.17 = f32[8,4,36,768]{3,2,0,1:T(8,128)S(1)} fusion(bf16[1,4,2048,768]{3,2,1,0:T(8,128)(2,1)} %param.10, bf16[8,4,36,2048]{3,2,1,0:T(8,128)(2,1)S(1)} %convolution_convert_fusion), kind=kOutput, calls=%fused_computation.21 | convolution fusion | flops 3623878656 | bytes 20840448 | tf_op jit(solution)/shard_map/secd,edf->secf/dot_general | solution.py:51
  175.0 0.0 slice-done.2
  175.0 7.4 %fusion.23 = (bf16[8,4,36,384]{3,2,0,1:T(8,128)(2,1)S(1)}, bf16[8,4,36,384]{3,2,0,1:T(8,128)(2,1)S(1)}) fusion(f32[8,4,36,768]{3,2,0,1:T(8,128)S(1)} %fusion.17, bf16[1,4,384,2048]{3,2,1,0:T(8,128)(2,1)} %param.11, bf16[8,4,36,2048]{3,2,1,0:T(8,128)(2,1)S(1)} %bitcast.78), kind=kOutput, calls=%fused_computation.26 | convolution fusion | flops 1817690112 | bytes 16318464 | tf_op jit(solution)/shard_map/secd,efd->secf/dot_general | solution.py:55
  182.5 14.5 %fusion.3 = bf16[4,8,36,2048]{3,2,0,1:T(8,128)(2,1)} fusion(bf16[1,4,2048,768]{3,2,1,0:T(8,128)(2,1)} %param.10, bf16[8,4,36,384]{3,2,0,1:T(8,128)(2,1)S(1)} %get-tuple-element.4, bf16[8,4,36,384]{3,2,0,1:T(8,128)(2,1)S(1)} %get-tuple-element.3), kind=kOutput, calls=%fused_computation.5 | convolution fusion | flops 3627417600 | bytes 19070976 | tf_op jit(solution)/shard_map/secf,edf->secd/dot_general | solution.py:57
  197.0 5.9 %bitcast_convert_fusion.2 = bf16[8,128,2048]{2,1,0:T(8,128)(2,1)} fusion(bf16[4,8,36,2048]{3,2,0,1:T(8,128)(2,1)} %fusion.3, f32[8,4,128]{2,1,0:T(4,128)S(1)} %fusion.40, f32[36]{0:T(128)S(1)} %iota_convert_fusion, pred[8,4,128]{2,1,0:T(4,128)(4,1)S(1)} %compare_reduce_fusion), kind=kOutput, calls=%fused_computation.8 | convolution fusion | flops 606371840 | bytes 8933520 | tf_op jit(solution)/shard_map/sect,secd->std/dot_general | solution.py:58
  202.9 4.9 %all-to-all-start = ((bf16[8,128,2048]{2,1,0:T(8,128)(2,1)}), bf16[8,128,2048]{2,1,0:T(8,128)(2,1)}, u32[]{:S(2)}, u32[]{:S(2)}) async-start(bf16[8,128,2048]{2,1,0:T(8,128)(2,1)} %bitcast_convert_fusion.2), calls=%async_computation | async-start | bytes 8388608 | tf_op jit(solution)/shard_map/all_to_all | solution.py:59
  207.8 0.0 slice-start.1
  207.9 10.2 %fusion.5 = bf16[1,4,384,2048]{3,2,1,0:T(8,128)(2,1)} fusion(bf16[8,4,36,2048]{3,2,1,0:T(8,128)(2,1)} %multiply_convert_fusion, f32[8,4,36,768]{3,2,0,1:T(8,128)} %copy-done.2), kind=kOutput, calls=%fused_computation.10 | convolution fusion | flops 1817739264 | bytes 14548992 | tf_op jit(solution)/shard_map/secf,secd->efd/dot_general | solution.py:60
  218.0 0.0 slice-done
  218.0 10.2 %fusion = bf16[1,4,2048,768]{3,2,1,0:T(8,128)(2,1)} fusion(bf16[8,4,36,2048]{3,2,1,0:T(8,128)(2,1)S(1)} %bitcast.76, bf16[8,4,36,384]{3,2,0,1:T(8,128)(2,1)S(1)} %get-tuple-element.4, bf16[8,4,36,384]{3,2,0,1:T(8,128)(2,1)S(1)} %get-tuple-element.3), kind=kOutput, calls=%fused_computation.1 | convolution fusion | flops 3633709056 | bytes 19070976 | tf_op jit(solution)/shard_map/secd,secf->edf/dot_general | solution.py:61
  228.2 71.7 %all-to-all-done = bf16[8,128,2048]{2,1,0:T(8,128)(2,1)} async-done(((bf16[8,128,2048]{2,1,0:T(8,128)(2,1)}), bf16[8,128,2048]{2,1,0:T(8,128)(2,1)}, u32[]{:S(2)}, u32[]{:S(2)}) %all-to-all-start) | async-done | bytes 4194336 | tf_op jit(solution)/shard_map/all_to_all | solution.py:59
  299.9 4.0 %convert_reduce_fusion = f32[128,2048]{1,0:T(8,128)} fusion(bf16[8,128,2048]{2,1,0:T(8,128)(2,1)} %all-to-all-done), kind=kLoop, calls=%fused_computation.9 | loop fusion | flops 3932160 | bytes 5242880 | tf_op jit(solution)/shard_map/reduce_sum | solution.py:62
  (16 shorter events, 0.1 us)
Async XLA Ops:
  7.2 79.6 %all-gather.5.cloned.1.call-start = ((), (), s32[]{:S(2)}) async-start(), calls=%async_computation.1 | async-start | bytes 4718592 | tf_op jit(solution)/shard_map/all_gather | solution.py:43
  7.9 153.4 %all-gather.7.cloned.1.call-start = ((), (), s32[]{:S(2)}) async-start(), calls=%async_computation.2 | async-start | bytes 4718592 | tf_op jit(solution)/shard_map/all_gather | solution.py:44
  7.9 15.1 %collective-permute-start = (bf16[128,2048]{1,0:T(8,128)(2,1)}, bf16[128,2048]{1,0:T(8,128)(2,1)S(1)}, u32[]{:S(2)}, u32[]{:S(2)}) collective-permute-start(bf16[128,2048]{1,0:T(8,128)(2,1)} %bitcast.84), channel_id=1, source_target_pairs={{0,24},{8,16},{16,8},{24,0},{1,25},{9,17},{17,9},{25,1},{2,26},{10... | collective-permute-start | bytes 1572872 | tf_op jit(solution)/shard_map/ppermute | solution.py:11
  23.0 0.8 copy-start.1
  161.3 13.6 %slice-start.2 = ((s8[5242880]{0:T(1024)(128)(4,1)}), s8[4194304]{0:T(1024)(128)(4,1)S(1)}, s32[]{:S(2)}) async-start(s8[5242880]{0:T(1024)(128)(4,1)} %bitcast.77), calls=%async_computation.5 | async-start | bytes 8388608
  165.2 2.3 copy-start
  167.5 7.5 %slice-start.3 = ((s8[5242880]{0:T(1024)(128)(4,1)}), s8[1048576]{0:T(1024)(128)(4,1)S(1)}, s32[]{:S(2)}) async-start(s8[5242880]{0:T(1024)(128)(4,1)} %bitcast.77), calls=%async_computation.6 | async-start | bytes 2097152
  175.0 7.5 %copy-start.2 = (f32[8,4,36,768]{3,2,0,1:T(8,128)}, f32[8,4,36,768]{3,2,0,1:T(8,128)S(1)}, u32[]{:S(2)}) copy-start(f32[8,4,36,768]{3,2,0,1:T(8,128)S(1)} %fusion.17) | copy-start | bytes 10616836
  202.9 15.1 %slice-start = ((s8[5242880]{0:T(1024)(128)(4,1)}), s8[1048576]{0:T(1024)(128)(4,1)S(1)}, s32[]{:S(2)}) async-start(s8[5242880]{0:T(1024)(128)(4,1)} %bitcast.75), calls=%async_computation.3 | async-start | bytes 2097152
  202.9 97.0 %all-to-all-start = ((bf16[8,128,2048]{2,1,0:T(8,128)(2,1)}), bf16[8,128,2048]{2,1,0:T(8,128)(2,1)}, u32[]{:S(2)}, u32[]{:S(2)}) async-start(bf16[8,128,2048]{2,1,0:T(8,128)(2,1)} %bitcast_convert_fusion.2), calls=%async_computation | async-start | bytes 8388608 | tf_op jit(solution)/shard_map/all_to_all | solution.py:59
  207.8 10.2 %slice-start.1 = ((s8[5242880]{0:T(1024)(128)(4,1)}), s8[4194304]{0:T(1024)(128)(4,1)S(1)}, s32[]{:S(2)}) async-start(s8[5242880]{0:T(1024)(128)(4,1)} %bitcast.75), calls=%async_computation.4 | async-start | bytes 8388608
Sparse Core Ops, SparseCore 0:
  10.1 76.5 all-gather.4
  89.5 71.8 all-gather.6
